TPU v7x, 32 devices: a whole 2x2x4 slice. The times are simulated.
32 devices in a mesh: clu: 16 (over z, y, core), col: 2 (over x).
Axes of the slice: x: 2, y: 2, z: 4, core: 2. Of those that a mesh axis runs over, the one named last changes fastest.
Arguments:
- near_blocks: float32 [16, 16, 512, 512], P('clu', 'col'), may hold values from -0.25 to 0.25
- diag_block: float32 [16, 512, 512], P('clu', 'col'), as said below
- bases: float32 [16, 512, 512], P('clu', 'col'), as said below
- near_index: int32 [16, 16], replicated, may hold values from 0 to 15, as said below
- near_mask: int32 [16, 16], P('clu'), may hold values from 0 to 1
- parent_map: int32 [16], replicated, may hold values from 0 to 7, as said below
Outputs:
- coupling: float32 [16, 16, 256, 256], P('clu', 'col')
- parent_rows: float32 [16, 256, 512], P('clu', 'col')
- redundant_factor: float32 [16, 256, 256], P('clu', 'col')
Inputs may be any that keep to these rules, and one draw needn't show every extreme that they name: `parent_map`: every parent has exactly two children. `near_index`: the slots of cluster i name the clusters (i + d) mod 16 for d = 1 to 7, d = 8 and d = -1 to -8, each offset in exactly one slot, in an order drawn per row; live slots name distinct clusters; exactly one live slot names the cluster's sibling. `diag_block`: each block is symmetric and positive definite. `bases`: each basis change is invertible.
All inputs are finite; a program needn't handle non-finite values.
Results may differ from a plain program's by a relative error of at most 0.0003.
Values sent between devices are 32-bit elements; how exact they have to be, the bound alone decides.
A program may use at most 64 MiB of HBM per device.

v0:
```python
import functools

import jax
import jax.numpy as jnp
from jax import lax
from jax.experimental import pallas as pl
from jax.experimental.pallas import tpu as pltpu
from jax.sharding import PartitionSpec as P

RANK = 256


def solve_lower(factor):
    size = factor.shape[0]
    return lax.linalg.triangular_solve(
        factor, jnp.eye(size, dtype=factor.dtype), left_side=True, lower=True
    )


def pick_rows(listed, carry, piece):
    count = piece.shape[0]
    select = (listed[:, None] == jnp.arange(count, dtype=jnp.int32)[None, :]).astype(jnp.float32)
    flat = piece.reshape(count, -1)
    return jnp.dot(select, flat, precision=lax.Precision.HIGHEST).reshape(carry.shape)


def shards(near_blocks, diag_block, bases, near_index, near_mask, parent_map):
    highest = lax.Precision.HIGHEST
    columns = lax.axis_size("col")
    column = lax.axis_index("col")
    own_index = lax.axis_index("clu")
    row_count = bases.shape[1]
    leaf_size = bases.shape[2]
    redundant = leaf_size - RANK
    per_device = near_blocks.shape[1]
    slot_total = near_index.shape[1]
    listed = lax.dynamic_slice_in_dim(near_index, own_index, 1, 0)[0]
    full_diag, full_basis = (
        lax.all_gather(diag_block, "col", axis=1, tiled=True),
        lax.all_gather(bases, "col", axis=1, tiled=True),
    )
    basis = full_basis[0]
    reduced = jnp.dot(basis.T, jnp.dot(full_diag[0], basis, precision=highest), precision=highest)
    factor = jnp.linalg.cholesky(reduced[:redundant, :redundant])
    inverse = solve_lower(factor)
    couple = jnp.dot(inverse, reduced[:redundant, redundant:], precision=highest)
    schur = reduced[redundant:, redundant:] - jnp.dot(couple.T, couple, precision=highest)
    skeleton_rows = bases[:, :, redundant:]
    empty = jnp.zeros((slot_total, row_count, RANK), jnp.float32)
    picked = pick_rows(listed, empty, lax.all_gather(skeleton_rows, "clu", axis=0, tiled=True))
    grouped = picked.reshape(columns, per_device, row_count, RANK)
    routed = lax.all_to_all(grouped, "col", split_axis=0, concat_axis=2, tiled=True)
    partners = routed[0]
    middle = jnp.einsum("kab,kbr->kar", near_blocks[0], partners, precision=highest)
    coupled = jnp.einsum("ba,kbr->kar", basis, middle, precision=highest)
    solved = jnp.einsum("xy,kyr->kxr", inverse, coupled[:, :redundant], precision=highest)
    local_list = lax.dynamic_slice_in_dim(listed, column * per_device, per_device, 0)
    local_live = lax.dynamic_slice_in_dim(near_mask[0], column * per_device, per_device, 0).astype(
        jnp.float32
    )
    coupling = (
        coupled[:, redundant:] - jnp.einsum("xs,kxr->ksr", couple, solved, precision=highest)
    ) * local_live[:, None, None]
    cluster_ids = jnp.arange(parent_map.shape[0], dtype=jnp.int32)
    own_parent = lax.dynamic_slice_in_dim(parent_map, own_index, 1, 0)[0]
    same = (parent_map == own_parent) & (cluster_ids != own_index)
    sibling = jnp.sum(jnp.where(same, cluster_ids, 0))
    matches = local_live * (local_list == sibling).astype(jnp.float32)
    side = jnp.einsum("k,kab->ab", matches, coupling, precision=highest)
    first = (own_index < sibling).astype(jnp.float32)
    side_wide = jnp.concatenate([(1.0 - first) * side, first * side], axis=1)
    summed = lax.psum_scatter(side_wide, "col", scatter_dimension=0, tiled=True)
    merged_count = summed.shape[0]
    schur_rows = lax.dynamic_slice_in_dim(schur, column * merged_count, merged_count, 0)
    parent_rows = summed + jnp.concatenate([first * schur_rows, (1.0 - first) * schur_rows], axis=1)
    factor_count = redundant // columns
    factor_rows = lax.dynamic_slice_in_dim(factor, column * factor_count, factor_count, 0)
    return (coupling[None], parent_rows[None], factor_rows[None])


ORDERS = (("z", "x", "y", "core"), ("z", "y", "x", "core"))
DIMS = ("z", "y", "core", "x")
HIGHEST = lax.Precision.HIGHEST
BLOCK = 64


def dot(a, b, contract=((1,), (0,))):
    return lax.dot_general(
        a, b, (contract, ((), ())), precision=HIGHEST, preferred_element_type=jnp.float32
    )


def halves(x):
    high = x.astype(jnp.bfloat16)
    return high, (x - high.astype(jnp.float32)).astype(jnp.bfloat16)


def dot_split(a, b):
    one = functools.partial(jnp.dot, preferred_element_type=jnp.float32)
    return one(a[0], b[0]) + (one(a[0], b[1]) + one(a[1], b[0]))


def fused(
    clusters,
    near_ref, diag_ref, bases_ref, index_ref, mask_ref, parent_ref,
    coupling_ref, rows_ref, factor_ref,
    every, near, peer_diag, peer_red, basis, system, small, t_high, t_low, wide, lower, schur,
    w_scr, side_out, side_in,
    send_sem, recv_sem, near_sem, pair_send, pair_recv,
):
    sizes = {"z": clusters // 4, "y": 2, "core": 2, "x": 2}
    clu, col = lax.axis_index("clu"), lax.axis_index("col")
    here = {"z": clu // 4, "y": lax.rem(clu // 2, 2), "core": lax.rem(clu, 2), "x": col}
    rows = bases_ref.shape[1]
    leaf = bases_ref.shape[2]
    red = leaf - RANK
    slots = near_ref.shape[1]
    parts = ((0, rows * 3 // 4), (rows * 3 // 4, rows - rows * 3 // 4))

    def place(coords):
        return ((coords["z"] * 2 + coords["y"]) * 2 + coords["core"], coords["x"])

    def moved(rel, sign):
        return place({
            d: here[d] if rel[i] == 0 else lax.rem(here[d] + (rel[i] * sign) % sizes[d], sizes[d])
            for i, d in enumerate(DIMS)
        })

    def number(rel):
        total = 0
        for d, r in zip(DIMS, rel):
            total = total * sizes[d] + r
        return total

    zero = (0, 0, 0, 0)

    def transfer(part, source, rel):
        step = tuple(b - a for a, b in zip(source, rel))
        origin = moved(source, -1)
        start, count = parts[part]
        piece = every.at[origin[0], pl.ds(pl.multiple_of(origin[1] * rows + start, 8), count)]
        return pltpu.make_async_remote_copy(
            src_ref=piece, dst_ref=piece,
            send_sem=send_sem.at[part, number(rel)], recv_sem=recv_sem.at[part, number(rel)],
            device_id=moved(step, 1), device_id_type=pl.DeviceIdType.MESH,
        )

    def arrival(part, rel):
        origin = moved(rel, -1)
        start, count = parts[part]
        piece = every.at[origin[0], pl.ds(pl.multiple_of(origin[1] * rows + start, 8), count)]
        step = tuple((1 if d == "x" else 0) for d in DIMS)
        return pltpu.make_async_remote_copy(
            src_ref=piece, dst_ref=piece,
            send_sem=send_sem.at[part, number(rel)], recv_sem=recv_sem.at[part, number(rel)],
            device_id=moved(step, 1), device_id_type=pl.DeviceIdType.MESH,
        )

    sent = []

    def children(part, rel):
        order = ORDERS[part]
        last = max([order.index(d) for d, r in zip(DIMS, rel) if r], default=-1)
        out = []
        for d in order[last + 1:]:
            for k in range(1, sizes[d]):
                out.append((d, tuple(k if e == d else r for e, r in zip(DIMS, rel))))
        return out

    def forward(part, rel, only=None):
        for d, child in children(part, rel):
            if only is None or d in only:
                copy = transfer(part, rel, child)
                copy.start()
                sent.append(copy)

    def pump(items):
        for part, rel in items:
            arrival(part, rel).wait_recv()
            forward(part, rel)

    unit = lambda d, k: tuple(k if e == d else 0 for e in DIMS)
    peers = [unit(d, k) for d in DIMS for k in range(1, sizes[d])]

    for k in range(slots):
        pltpu.make_async_copy(near_ref.at[0, k], near.at[k], near_sem.at[k]).start()

    barrier = pltpu.get_barrier_semaphore()
    for rel in peers:
        pl.semaphore_signal(barrier, inc=1, device_id=moved(rel, 1), device_id_type=pl.DeviceIdType.MESH)
    every[clu, pl.ds(pl.multiple_of(col * rows, 8), rows), :] = bases_ref[0, :, red:]
    pl.semaphore_wait(barrier, len(peers))

    across = moved(unit("x", 1), 1)

    def pair(i, src, dst):
        return pltpu.make_async_remote_copy(
            src_ref=src, dst_ref=dst, send_sem=pair_send.at[i], recv_sem=pair_recv.at[i],
            device_id=across, device_id_type=pl.DeviceIdType.MESH,
        )

    red_copy = pair(0, bases_ref.at[0, :, pl.ds(0, red)], peer_red)
    diag_copy = pair(
        1, diag_ref.at[0, :, pl.ds(pl.multiple_of(col * rows, 128), rows)], peer_diag
    )
    red_copy.start()
    diag_copy.start()
    for part in range(2):
        forward(part, zero, ("x",))
    for part in range(2):
        forward(part, zero, ("z", "y", "core"))

    plain = [
        (part, rel)
        for rel in [
            (z, y, 0, x) for z in range(sizes["z"]) for y in range(2) for x in range(2)
        ]
        for part in range(2)
        if any(rel)
    ]
    level = lambda item: sum(1 for r in item[1] if r)
    ones = sorted([i for i in plain if level(i) == 1], key=lambda i: (-i[1][3], i[1][1]))
    twos = [i for i in plain if level(i) == 2]
    threes = [i for i in plain if level(i) == 3]

    red_copy.wait_recv()
    diag_copy.wait_recv()
    pump(ones)
    basis[:rows] = bases_ref[0]
    basis[rows:, :red] = peer_red[...]
    basis[rows:, red:] = every[clu, pl.ds(pl.multiple_of((1 - col) * rows, 8), rows), :]
    own = diag_ref[0, :, pl.ds(pl.multiple_of(col * rows, 128), rows)]
    off = diag_ref[0, :, pl.ds(pl.multiple_of((1 - col) * rows, 128), rows)]
    wide[:rows] = dot(own, basis[:rows]) + dot(off, basis[rows:])
    wide[rows:] = dot(off.T, basis[:rows]) + dot(peer_diag[...], basis[rows:])
    system[:, : red + RANK] = dot(basis[:, :red], wide[...], ((0,), (0,)))
    schur[...] = dot(basis[:, red:], wide[:, red:], ((0,), (0,)))
    row_id = lax.broadcasted_iota(jnp.int32, (red, red), 0)
    col_id = lax.broadcasted_iota(jnp.int32, (red, red), 1)
    system[:, red + RANK:] = (row_id == col_id).astype(jnp.float32)

    steps = red // BLOCK
    share = -(-len(twos) // steps)
    sub = lax.broadcasted_iota(jnp.int32, (BLOCK, 2 * BLOCK), 0)
    lane = lax.broadcasted_iota(jnp.int32, (BLOCK, 2 * BLOCK), 1)
    unit_right = (sub + BLOCK == lane).astype(jnp.float32)
    for b in range(steps):
        low, high = b * BLOCK, (b + 1) * BLOCK
        small[...] = jnp.concatenate(
            [system[low:high, low:high], unit_right[:, BLOCK:]], axis=1
        )

        def eliminate(j, _):
            block = small[...]
            row = small[pl.ds(j, 1), :]
            column = jnp.sum(jnp.where(lane == j, block, 0.0), axis=1, keepdims=True)
            pivot = jnp.sum(jnp.where(lane[:1] == j, row, 0.0), axis=1, keepdims=True)
            scaled = row / pivot
            small[...] = block - jnp.where(sub > j, column, 0.0) * scaled
            return 0

        lax.fori_loop(0, BLOCK, eliminate, 0)
        done = small[...]
        pivots = jnp.sum(jnp.where(sub == lane, done, 0.0), axis=1, keepdims=True)
        inverse = done[:, BLOCK:] / jnp.sqrt(pivots)
        solved = dot(inverse, system[low:high, :])
        upper = jnp.where(
            col_id[low:high] >= row_id[low:high], solved[:, :red], 0.0
        )
        system[low:high, :red] = upper
        system[low:high, red:] = solved[:, red:]
        if high < red:
            system[high:, :] -= dot(
                upper[:, high:], jnp.concatenate([upper, solved[:, red:]], axis=1), ((0,), (0,))
            )
        pump(twos[b * share:(b + 1) * share])
    pump(threes)

    lower[...] = system[:, :red].T
    half = red // 2
    factor_ref[0] = lower[pl.ds(pl.multiple_of(col * half, 8), half), :]
    couple = system[:, red:red + RANK]
    schur[...] -= dot(couple, couple, ((0,), (0,)))
    middle = dot(system[:, red + RANK:], couple, ((0,), (0,)))
    w_scr[pl.ds(pl.multiple_of(col * rows, 8), rows), :] = (
        basis[:rows, red:] - dot(basis[:rows, :red], middle)
    )
    w_scr[pl.ds(pl.multiple_of((1 - col) * rows, 8), rows), :] = (
        basis[rows:, red:] - dot(basis[rows:, :red], middle)
    )
    turned = halves(w_scr[...].T)

    parent = parent_ref[clu]
    sibling = jnp.int32(0)
    for c in range(clusters):
        sibling = jnp.where((parent_ref[c] == parent) & (c != clu), jnp.int32(c), sibling)

    wide[:RANK] = jnp.zeros((RANK, leaf), jnp.float32)
    for k in range(slots):
        pltpu.make_async_copy(near_ref.at[0, k], near.at[k], near_sem.at[k]).wait()

    def project(k, _):
        value = dot_split(turned, halves(near[k]))
        t_high[k], t_low[k] = halves(value)
        slot = col * slots + k
        match = jnp.where(index_ref[clu, slot] == sibling, mask_ref[0, slot], 0)
        wide[:RANK] += value * match.astype(jnp.float32)
        return 0

    lax.fori_loop(0, slots, project, 0)

    for part in range(2):
        for rel in [(z, y, 1, x) for z in range(sizes["z"]) for y in range(2) for x in range(2)]:
            arrival(part, rel).wait_recv()
    side = dot_split(halves(wide[:RANK]), halves(every[sibling]))
    quarter = RANK // 2
    side_out[...] = side
    side_copy = pair(
        2, side_out.at[pl.ds(pl.multiple_of((1 - col) * quarter, 8), quarter)], side_in
    )
    side_copy.start()

    def finish(k, _):
        slot = col * slots + k
        live = mask_ref[0, slot].astype(jnp.float32)
        coupling_ref[0, k] = live * dot_split(
            (t_high[k], t_low[k]), halves(every[index_ref[clu, slot]])
        )
        return 0

    lax.fori_loop(0, slots, finish, 0)
    side_copy.wait_recv()
    mine = pl.ds(pl.multiple_of(col * quarter, 8), quarter)
    side_rows = side_out[mine, :] + side_in[...]
    schur_rows = schur[mine, :]
    first = (clu < sibling).astype(jnp.float32)
    rows_ref[0, :, :RANK] = first * schur_rows + (1.0 - first) * side_rows
    rows_ref[0, :, RANK:] = (1.0 - first) * schur_rows + first * side_rows
    for copy in sent + [red_copy, diag_copy, side_copy]:
        copy.wait_send()


def fused_shards(near_blocks, diag_block, bases, near_index, near_mask, parent_map):
    clusters = parent_map.shape[0]
    rows, leaf = bases.shape[1:]
    red = leaf - RANK
    slots = near_blocks.shape[1]
    f32, b16 = jnp.float32, jnp.bfloat16
    vmem = pl.BlockSpec(memory_space=pltpu.VMEM)
    smem = pl.BlockSpec(memory_space=pltpu.SMEM)
    dma = pltpu.SemaphoreType.DMA
    devices = clusters * 2
    return pl.pallas_call(
        functools.partial(fused, clusters),
        out_shape=(
            jax.ShapeDtypeStruct((1, slots, RANK, RANK), f32),
            jax.ShapeDtypeStruct((1, RANK // 2, 2 * RANK), f32),
            jax.ShapeDtypeStruct((1, red // 2, red), f32),
        ),
        in_specs=[pl.BlockSpec(memory_space=pl.ANY), vmem, vmem, smem, smem, smem],
        out_specs=(vmem, vmem, vmem),
        scratch_shapes=[
            pltpu.VMEM((clusters, leaf, RANK), f32),
            pltpu.VMEM((slots, leaf, leaf), f32),
            pltpu.VMEM((rows, rows), f32),
            pltpu.VMEM((rows, red), f32),
            pltpu.VMEM((leaf, leaf), f32),
            pltpu.VMEM((red, 2 * red + RANK), f32),
            pltpu.VMEM((BLOCK, 2 * BLOCK), f32),
            pltpu.VMEM((slots, RANK, leaf), b16),
            pltpu.VMEM((slots, RANK, leaf), b16),
            pltpu.VMEM((leaf, leaf), f32),
            pltpu.VMEM((red, red), f32),
            pltpu.VMEM((RANK, RANK), f32),
            pltpu.VMEM((leaf, RANK), f32),
            pltpu.VMEM((RANK, RANK), f32),
            pltpu.VMEM((RANK // 2, RANK), f32),
            dma((2, devices)),
            dma((2, devices)),
            dma((slots,)),
            dma((3,)),
            dma((3,)),
        ],
        compiler_params=pltpu.CompilerParams(
            collective_id=0, has_side_effects=True, vmem_limit_bytes=48 * 1024 * 1024
        ),
    )(near_blocks, diag_block, bases, near_index, near_mask, parent_map)


def solution(mesh):
    in_specs = (
        P("clu", "col", None, None),
        P("clu", "col", None),
        P("clu", "col", None),
        P(),
        P("clu", None),
        P(),
    )
    out_specs = (P("clu", "col", None, None), P("clu", "col", None), P("clu", "col", None))
    pairs = mesh.shape["col"] == 2 and mesh.shape["clu"] % 4 == 0
    body = fused_shards if pairs else shards
    return jax.shard_map(body, mesh=mesh, in_specs=in_specs, out_specs=out_specs, check_vma=False)
```

profile of v0, /device:TPU:0, one launch (start us, length us, event | category | flops | bytes accessed | tf_op | source)
XLA Modules:
  0.0 86.9 jit_solution(15594032679761996856)
XLA Ops:
  0.6 0.0 copy-start
  0.6 1.0 %copy-done = f32[1,256,512]{2,1,0:T(8,128)S(1)} copy-done((f32[1,256,512]{2,1,0:T(8,128)S(1)}, f32[1,256,512]{2,1,0:T(8,128)}, u32[]{:S(2)}) %copy-start) | copy-done | bytes 524312
  1.7 0.0 copy-start.1
  1.7 1.0 %copy-done.1 = f32[1,256,512]{2,1,0:T(8,128)S(1)} copy-done((f32[1,256,512]{2,1,0:T(8,128)S(1)}, f32[1,256,512]{2,1,0:T(8,128)}, u32[]{:S(2)}) %copy-start.1) | copy-done | bytes 524312
  2.7 0.0 copy-start.2
  2.7 0.7 copy-done.2
  3.4 0.0 copy-start.3
  3.4 0.7 copy-done.3
  4.1 0.0 copy-start.4
  4.1 0.7 copy-done.4
  4.7 79.5 %shard_map.85 = (f32[1,8,256,256]{3,2,1,0:T(8,128)S(1)}, f32[1,128,512]{2,1,0:T(8,128)S(1)}, f32[1,128,256]{2,1,0:T(8,128)S(1)}) custom-call(f32[1,8,512,512]{3,2,1,0:T(8,128)} %near_ref.1, f32[1,256,512]{2,1,0:T(8,128)S(1)} %copy-done, f32[1,256,512]{2,1,0:T(8,128)S(1)} %copy-done.1, s32[16,16]{1,0:T(8,128)S(1)} %copy-done.2, s32[1,16]{1,0:T(1,128)S(1)} %copy-done.3, ...), custom_call_target="tpu_custom_call" | custom-call | tf_op jit(solution)/shard_map/pallas_call | solution.py:353
  84.3 1.3 %copy.12 = f32[1,8,256,256]{3,2,1,0:T(8,128)} copy(f32[1,8,256,256]{3,2,1,0:T(8,128)S(1)} %get-tuple-element.6) | data formatting | bytes 4194304
  85.6 0.7 copy.13
  86.3 0.7 copy.14
Async XLA Ops:
  0.6 1.0 %copy-start = (f32[1,256,512]{2,1,0:T(8,128)S(1)}, f32[1,256,512]{2,1,0:T(8,128)}, u32[]{:S(2)}) copy-start(f32[1,256,512]{2,1,0:T(8,128)} %diag_ref.1) | copy-start | bytes 1572868
  1.7 1.0 %copy-start.1 = (f32[1,256,512]{2,1,0:T(8,128)S(1)}, f32[1,256,512]{2,1,0:T(8,128)}, u32[]{:S(2)}) copy-start(f32[1,256,512]{2,1,0:T(8,128)} %bases_ref.1) | copy-start | bytes 1572868
  2.7 0.7 copy-start.2
  3.4 0.7 copy-start.3
  4.1 0.7 copy-start.4
where the time goes:
time: 87.2 us; the launch traced here: 86.9 us
  Pallas kernels  79.5 us (91%)
  local copies, waits for them, and re-layouts  6.76 us (8%)
    pallas_call x1, Pallas kernels, fused_shards(): pl.pallas_call(functools.partial(fused, clusters), out_shape=(jax.ShapeDt...  79.5 us
    unnamed x13, local copies, waits for them, and re-layouts  6.76 us

commit v1 on v0

--- a/solution.py
+++ b/solution.py
@@ -104,7 +104,7 @@
     clusters,
     near_ref, diag_ref, bases_ref, index_ref, mask_ref, parent_ref,
     coupling_ref, rows_ref, factor_ref,
-    every, near, peer_diag, peer_red, basis, system, small, t_high, t_low, wide, lower, schur,
+    every, near, peer_diag, peer_red, basis, system, t_high, t_low, wide, lower, schur,
     w_scr, side_out, side_in,
     send_sem, recv_sem, near_sem, pair_send, pair_recv,
 ):
@@ -246,21 +246,11 @@
     unit_right = (sub + BLOCK == lane).astype(jnp.float32)
     for b in range(steps):
         low, high = b * BLOCK, (b + 1) * BLOCK
-        small[...] = jnp.concatenate(
-            [system[low:high, low:high], unit_right[:, BLOCK:]], axis=1
-        )
-
-        def eliminate(j, _):
-            block = small[...]
-            row = small[pl.ds(j, 1), :]
-            column = jnp.sum(jnp.where(lane == j, block, 0.0), axis=1, keepdims=True)
-            pivot = jnp.sum(jnp.where(lane[:1] == j, row, 0.0), axis=1, keepdims=True)
-            scaled = row / pivot
-            small[...] = block - jnp.where(sub > j, column, 0.0) * scaled
-            return 0
-
-        lax.fori_loop(0, BLOCK, eliminate, 0)
-        done = small[...]
+        done = jnp.concatenate([system[low:high, low:high], unit_right[:, BLOCK:]], axis=1)
+        for j in range(BLOCK - 1):
+            column = done[:, j:j + 1]
+            scaled = done[j:j + 1, :] / done[j:j + 1, j:j + 1]
+            done = done - jnp.where(sub > j, column, 0.0) * scaled
         pivots = jnp.sum(jnp.where(sub == lane, done, 0.0), axis=1, keepdims=True)
         inverse = done[:, BLOCK:] / jnp.sqrt(pivots)
         solved = dot(inverse, system[low:high, :])
@@ -366,7 +356,6 @@
             pltpu.VMEM((rows, red), f32),
             pltpu.VMEM((leaf, leaf), f32),
             pltpu.VMEM((red, 2 * red + RANK), f32),
-            pltpu.VMEM((BLOCK, 2 * BLOCK), f32),
             pltpu.VMEM((slots, RANK, leaf), b16),
             pltpu.VMEM((slots, RANK, leaf), b16),
             pltpu.VMEM((leaf, leaf), f32),

time: 87.2 us -> 84.5 us (0.969)
  Pallas kernels: 79.5 us -> 76.8 us
    pallas_call x1, Pallas kernels: 79.5 us -> 76.8 us  [fused_shards(): pl.pallas_call(functools.partial(fused, clusters), out_shape=(jax.ShapeDt...]
where the time goes in v1:
time: 84.5 us; the launch traced here: 84.2 us
  Pallas kernels  76.8 us (91%)
  local copies, waits for them, and re-layouts  6.76 us (8%)
    pallas_call x1, Pallas kernels, fused_shards(): pl.pallas_call(functools.partial(fused, clusters), out_shape=(jax.ShapeDt...  76.8 us
    unnamed x13, local copies, waits for them, and re-layouts  6.76 us

profile of v1, /device:TPU:0, one launch (start us, length us, event | category | flops | bytes accessed | tf_op | source)
XLA Modules:
  0.0 84.2 jit_solution(9957320065394281158)
XLA Ops:
  0.6 0.0 copy-start
  0.6 1.0 %copy-done = f32[1,256,512]{2,1,0:T(8,128)S(1)} copy-done((f32[1,256,512]{2,1,0:T(8,128)S(1)}, f32[1,256,512]{2,1,0:T(8,128)}, u32[]{:S(2)}) %copy-start) | copy-done | bytes 524312
  1.7 0.0 copy-start.1
  1.7 1.0 %copy-done.1 = f32[1,256,512]{2,1,0:T(8,128)S(1)} copy-done((f32[1,256,512]{2,1,0:T(8,128)S(1)}, f32[1,256,512]{2,1,0:T(8,128)}, u32[]{:S(2)}) %copy-start.1) | copy-done | bytes 524312
  2.7 0.0 copy-start.2
  2.7 0.7 copy-done.2
  3.4 0.0 copy-start.3
  3.4 0.7 copy-done.3
  4.1 0.0 copy-start.4
  4.1 0.7 copy-done.4
  4.7 76.8 %shard_map.85 = (f32[1,8,256,256]{3,2,1,0:T(8,128)S(1)}, f32[1,128,512]{2,1,0:T(8,128)S(1)}, f32[1,128,256]{2,1,0:T(8,128)S(1)}) custom-call(f32[1,8,512,512]{3,2,1,0:T(8,128)} %near_ref.1, f32[1,256,512]{2,1,0:T(8,128)S(1)} %copy-done, f32[1,256,512]{2,1,0:T(8,128)S(1)} %copy-done.1, s32[16,16]{1,0:T(8,128)S(1)} %copy-done.2, s32[1,16]{1,0:T(1,128)S(1)} %copy-done.3, ...), custom_call_target="tpu_custom_call" | custom-call | tf_op jit(solution)/shard_map/pallas_call | solution.py:343
  81.5 1.3 %copy.12 = f32[1,8,256,256]{3,2,1,0:T(8,128)} copy(f32[1,8,256,256]{3,2,1,0:T(8,128)S(1)} %get-tuple-element.6) | data formatting | bytes 4194304
  82.8 0.7 copy.13
  83.5 0.7 copy.14
Async XLA Ops:
  0.6 1.0 %copy-start = (f32[1,256,512]{2,1,0:T(8,128)S(1)}, f32[1,256,512]{2,1,0:T(8,128)}, u32[]{:S(2)}) copy-start(f32[1,256,512]{2,1,0:T(8,128)} %diag_ref.1) | copy-start | bytes 1572868
  1.7 1.0 %copy-start.1 = (f32[1,256,512]{2,1,0:T(8,128)S(1)}, f32[1,256,512]{2,1,0:T(8,128)}, u32[]{:S(2)}) copy-start(f32[1,256,512]{2,1,0:T(8,128)} %bases_ref.1) | copy-start | bytes 1572868
  2.7 0.7 copy-start.2
  3.4 0.7 copy-start.3
  4.1 0.7 copy-start.4

commit v2 on v1

--- a/solution.py
+++ b/solution.py
@@ -247,10 +247,19 @@
     for b in range(steps):
         low, high = b * BLOCK, (b + 1) * BLOCK
         done = jnp.concatenate([system[low:high, low:high], unit_right[:, BLOCK:]], axis=1)
-        for j in range(BLOCK - 1):
-            column = done[:, j:j + 1]
-            scaled = done[j:j + 1, :] / done[j:j + 1, j:j + 1]
-            done = done - jnp.where(sub > j, column, 0.0) * scaled
+        for j in range(0, BLOCK, 2):
+            left = jnp.broadcast_to(done[:, j:j + 1], done.shape)
+            right = jnp.broadcast_to(done[:, j + 1:j + 2], done.shape)
+            pivot = left[j:j + 1, :]
+            scaled = done[j:j + 1, :] / pivot
+            right = right - left * (right[j:j + 1, :] / pivot)
+            second = done[j + 1:j + 2, :] - left[j + 1:j + 2, :] * scaled
+            second = second / right[j + 1:j + 2, :]
+            done = (
+                done
+                - jnp.where(sub > j, left, 0.0) * scaled
+                - jnp.where(sub > j + 1, right, 0.0) * second
+            )
         pivots = jnp.sum(jnp.where(sub == lane, done, 0.0), axis=1, keepdims=True)
         inverse = done[:, BLOCK:] / jnp.sqrt(pivots)
         solved = dot(inverse, system[low:high, :])

time: 84.5 us -> 78.3 us (0.927)
  Pallas kernels: 76.8 us -> 70.7 us
    pallas_call x1, Pallas kernels: 76.8 us -> 70.7 us  [fused_shards(): pl.pallas_call(functools.partial(fused, clusters), out_shape=(jax.ShapeDt...]
where the time goes in v2:
time: 78.3 us; the launch traced here: 78.1 us
  Pallas kernels  70.7 us (90%)
  local copies, waits for them, and re-layouts  6.76 us (9%)
    pallas_call x1, Pallas kernels, fused_shards(): pl.pallas_call(functools.partial(fused, clusters), out_shape=(jax.ShapeDt...  70.7 us
    unnamed x13, local copies, waits for them, and re-layouts  6.76 us

profile of v2, /device:TPU:0, one launch (start us, length us, event | category | flops | bytes accessed | tf_op | source)
XLA Modules:
  0.0 78.1 jit_solution(203627489085399154)
XLA Ops:
  0.6 0.0 copy-start
  0.6 1.0 %copy-done = f32[1,256,512]{2,1,0:T(8,128)S(1)} copy-done((f32[1,256,512]{2,1,0:T(8,128)S(1)}, f32[1,256,512]{2,1,0:T(8,128)}, u32[]{:S(2)}) %copy-start) | copy-done | bytes 524312
  1.7 0.0 copy-start.1
  1.7 1.0 %copy-done.1 = f32[1,256,512]{2,1,0:T(8,128)S(1)} copy-done((f32[1,256,512]{2,1,0:T(8,128)S(1)}, f32[1,256,512]{2,1,0:T(8,128)}, u32[]{:S(2)}) %copy-start.1) | copy-done | bytes 524312
  2.7 0.0 copy-start.2
  2.7 0.7 copy-done.2
  3.4 0.0 copy-start.3
  3.4 0.7 copy-done.3
  4.1 0.0 copy-start.4
  4.1 0.7 copy-done.4
  4.7 70.7 %shard_map.85 = (f32[1,8,256,256]{3,2,1,0:T(8,128)S(1)}, f32[1,128,512]{2,1,0:T(8,128)S(1)}, f32[1,128,256]{2,1,0:T(8,128)S(1)}) custom-call(f32[1,8,512,512]{3,2,1,0:T(8,128)} %near_ref.1, f32[1,256,512]{2,1,0:T(8,128)S(1)} %copy-done, f32[1,256,512]{2,1,0:T(8,128)S(1)} %copy-done.1, s32[16,16]{1,0:T(8,128)S(1)} %copy-done.2, s32[1,16]{1,0:T(1,128)S(1)} %copy-done.3, ...), custom_call_target="tpu_custom_call" | custom-call | tf_op jit(solution)/shard_map/pallas_call | solution.py:352
  75.4 1.3 %copy.12 = f32[1,8,256,256]{3,2,1,0:T(8,128)} copy(f32[1,8,256,256]{3,2,1,0:T(8,128)S(1)} %get-tuple-element.6) | data formatting | bytes 4194304
  76.7 0.7 copy.13
  77.4 0.7 copy.14
Async XLA Ops:
  0.6 1.0 %copy-start = (f32[1,256,512]{2,1,0:T(8,128)S(1)}, f32[1,256,512]{2,1,0:T(8,128)}, u32[]{:S(2)}) copy-start(f32[1,256,512]{2,1,0:T(8,128)} %diag_ref.1) | copy-start | bytes 1572868
  1.7 1.0 %copy-start.1 = (f32[1,256,512]{2,1,0:T(8,128)S(1)}, f32[1,256,512]{2,1,0:T(8,128)}, u32[]{:S(2)}) copy-start(f32[1,256,512]{2,1,0:T(8,128)} %bases_ref.1) | copy-start | bytes 1572868
  2.7 0.7 copy-start.2
  3.4 0.7 copy-start.3
  4.1 0.7 copy-start.4
